TPU v7x, 256 devices: a whole 4x4x8 slice. The times are simulated.
256 devices in a mesh: ctx: 8 (over z_hi, y), exp: 32 (over z_lo, x, core).
Axes of the slice: x: 4, y: 4, z: 8 (z_hi: 2, z_lo: 4; z = z_hi * 4 + z_lo), core: 2. Of those that a mesh axis runs over, the one named last changes fastest.
Arguments:
- query_rows: bfloat16 [32, 1024, 2048], P('exp', 'ctx'), may hold values from -5 to 5
- key_rows: bfloat16 [32, 1024, 256], P('exp', 'ctx'), may hold values from -5 to 5
- value_rows: bfloat16 [32, 1024, 256], P('exp', 'ctx'), may hold values from -6 to 6
- residual: bfloat16 [32, 1024, 2048], P('exp', None, 'ctx'), may hold values from -6 to 6
- out_weight: bfloat16 [2048, 2048], P(None, 'ctx'), may hold values from -0.125 to 0.125
- norm_gain: float32 [2048], P('ctx'), may hold values from 0.25 to 1.75
- gate_up: bfloat16 [256, 2048, 768], P(('ctx', 'exp')), may hold values from -0.125 to 0.125
- down_proj: bfloat16 [256, 384, 2048], P(('ctx', 'exp')), may hold values from -0.21875 to 0.21875
- expert_ids: int32 [32, 1024, 8], P('exp'), may hold values from 0 to 127, all different within a row; in each aligned block of 1024 rows (0 to 1023, 1024 to 2047, ..., all dimensions but the last counted through in order) at most 76 rows name the same one
- gate_vals: float32 [32, 1024, 8], P('exp'), may hold values from 0.02 to 0.3
Outputs:
- layer_out: bfloat16 [32, 1024, 2048], P('exp', None, 'ctx')
Inputs may be any that keep to these rules, and one draw needn't show every extreme that they name: `expert_ids`: the entries of one position name different experts. In each sequence no expert is named by more than 76 entries, and in some sequence one expert is named by exactly 76.
All inputs are finite; a program needn't handle non-finite values.
Results may differ from a plain program's by a relative error of at most 0.009.
Values may be sent and summed in bfloat16 or wider, within the bound.
A program may use at most 128 MiB of HBM per device.

v0:
```python
import jax
import jax.numpy as jnp
from jax import lax
from jax.sharding import PartitionSpec as P

D = 2048
HEAD = 128


neg_large = -1e30
norm_eps = 1e-06


def passed_along(value, axis, by):
    size = lax.axis_size(axis)
    pairs = [(i, i + by) for i in range(size) if 0 <= i + by < size]
    return lax.ppermute(value, axis, pairs)


def attend_block(
    state, block_keys, block_values, first_row, queries_grouped, query_pos, scale_factor
):
    row_count = block_keys.shape[0]
    kv_heads = queries_grouped.shape[1]
    keys_grouped = block_keys.reshape(row_count, kv_heads, -1)
    values_grouped = block_values.reshape(row_count, kv_heads, -1)
    scores = (
        jnp.einsum(
            "qkgd,tkd->qkgt", queries_grouped, keys_grouped, preferred_element_type=jnp.float32
        )
        * scale_factor
    )
    key_pos = first_row + jnp.arange(row_count, dtype=jnp.int32)
    allowed = (key_pos[None, :] <= query_pos[:, None])[:, None, None, :]
    scores = jnp.where(allowed, scores, neg_large)
    run_max, run_sum, accumulated = state
    new_max = jnp.maximum(run_max, jnp.max(scores, axis=-1))
    factor = jnp.exp(run_max - new_max)
    weights = jnp.where(allowed, jnp.exp(scores - new_max[..., None]), 0.0)
    run_sum = run_sum * factor + jnp.sum(weights, axis=-1)
    accumulated = accumulated * factor[..., None] + jnp.einsum(
        "qkgt,tkd->qkgd",
        weights.astype(jnp.bfloat16),
        values_grouped,
        preferred_element_type=jnp.float32,
    )
    return (new_max, run_sum, accumulated)


def shards(
    query_rows,
    key_rows,
    value_rows,
    residual,
    out_weight,
    norm_gain,
    gate_up,
    down_proj,
    expert_ids,
    gate_vals,
):
    ctx_index = lax.axis_index("ctx")
    ctx_count = lax.axis_size("ctx")
    group_size = lax.axis_size("exp")
    tok_rows = query_rows.shape[1]
    kv_heads = key_rows.shape[2] // HEAD
    queries_grouped = query_rows[0].reshape(tok_rows, kv_heads, -1, HEAD)
    per_group = queries_grouped.shape[2]
    query_pos = ctx_index * tok_rows + jnp.arange(tok_rows, dtype=jnp.int32)
    scale_factor = HEAD ** (-0.5)
    initial = (
        jnp.full((tok_rows, kv_heads, per_group), neg_large, jnp.float32),
        jnp.zeros((tok_rows, kv_heads, per_group), jnp.float32),
        jnp.zeros((tok_rows, kv_heads, per_group, HEAD), jnp.float32),
    )
    stacked = jnp.stack([key_rows[0], value_rows[0]])
    state = attend_block(
        initial,
        stacked[0],
        stacked[1],
        ctx_index * tok_rows,
        queries_grouped,
        query_pos,
        scale_factor,
    )

    def cycle_turn(turn, carry):
        state_now, moving = carry
        moving = passed_along(moving, "ctx", 1)
        source = (ctx_index - turn) % ctx_count
        state_now = attend_block(
            state_now,
            moving[0],
            moving[1],
            source * tok_rows,
            queries_grouped,
            query_pos,
            scale_factor,
        )
        return (state_now, moving)

    state, stacked = lax.fori_loop(1, ctx_count, cycle_turn, (state, stacked))
    run_max, run_sum, accumulated = state
    context = (accumulated / run_sum[..., None]).reshape(tok_rows, -1).astype(jnp.bfloat16)
    attn_cols = jnp.dot(
        lax.all_gather(context, "ctx", axis=0, tiled=True),
        out_weight,
        preferred_element_type=jnp.float32,
    )
    hidden_state = residual[0].astype(jnp.float32) + attn_cols
    square_part = jnp.sum(hidden_state * hidden_state, axis=1)
    square_total = lax.psum(square_part, "ctx")
    inv_rms = lax.rsqrt(square_total / D + norm_eps)
    normed_cols = (hidden_state * inv_rms[:, None] * norm_gain[None, :]).astype(jnp.bfloat16)
    normed = lax.all_gather(normed_cols, "ctx", axis=1, tiled=True)
    seq_len = normed.shape[0]
    width = normed.shape[1]
    capacity = 2 * (19 * tok_rows // (2 * group_size))
    my_class = ctx_index // 2
    flat_ids = expert_ids[0].reshape(-1)
    flat_gates = gate_vals[0].reshape(-1)
    pair_token = jnp.arange(flat_ids.shape[0], dtype=jnp.int32) // expert_ids.shape[2]
    is_mine = flat_ids // group_size == my_class
    target = flat_ids % group_size
    onehot = jnp.logical_and(
        target[:, None] == jnp.arange(group_size, dtype=jnp.int32)[None, :], is_mine[:, None]
    ).astype(jnp.int32)
    ranks = jnp.sum(jnp.cumsum(onehot, axis=0) * onehot, axis=1) - 1
    target = jnp.where(is_mine, target, group_size)
    token_table = (
        jnp.full((group_size, capacity), seq_len, jnp.int32)
        .at[target, ranks]
        .set(pair_token, mode="drop")
    )
    gate_table = (
        jnp.zeros((group_size, capacity), jnp.float32)
        .at[target, ranks]
        .set(flat_gates, mode="drop")
    )
    padded = jnp.concatenate([normed, jnp.zeros((1, width), jnp.bfloat16)], axis=0)
    outgoing = padded[token_table]
    received = lax.all_to_all(outgoing, "exp", split_axis=0, concat_axis=0, tiled=True)
    flat_rows = received.reshape(-1, width)
    gate_up_out = jnp.dot(flat_rows, gate_up[0], preferred_element_type=jnp.float32)
    half_width = down_proj.shape[1]
    hidden_units = (jax.nn.silu(gate_up_out[:, :half_width]) * gate_up_out[:, half_width:]).astype(
        jnp.bfloat16
    )
    expert_out = (
        jnp.dot(hidden_units, down_proj[0], preferred_element_type=jnp.float32)
        .astype(jnp.bfloat16)
        .reshape(received.shape)
    )
    returned = lax.all_to_all(expert_out, "exp", split_axis=0, concat_axis=0, tiled=True)
    weighted = returned.astype(jnp.float32) * gate_table[:, :, None]
    partial_sum = jax.ops.segment_sum(
        weighted.reshape(-1, width), token_table.reshape(-1), num_segments=seq_len + 1
    )[:seq_len]
    moe_cols = lax.psum_scatter(
        partial_sum.astype(jnp.bfloat16), "ctx", scatter_dimension=1, tiled=True
    ).astype(jnp.float32)
    return (hidden_state + moe_cols).astype(jnp.bfloat16)[None]


def solution(mesh):
    return jax.shard_map(
        shards,
        mesh=mesh,
        in_specs=(
            P("exp", "ctx", None),
            P("exp", "ctx", None),
            P("exp", "ctx", None),
            P("exp", None, "ctx"),
            P(None, "ctx"),
            P("ctx"),
            P(("ctx", "exp"), None, None),
            P(("ctx", "exp"), None, None),
            P("exp", None, None),
            P("exp", None, None),
        ),
        out_specs=P("exp", None, "ctx"),
        check_vma=False,
    )
```

profile of v0, /device:TPU:97, one launch (start us, length us, event | category | flops | bytes accessed | tf_op | source)
XLA Modules:
  0.0 1163.8 jit_solution(10173571608206733345)
XLA Ops:
  17.7 89.7 %while.22 = (s32[]{:T(128)}, f32[128,2,8]{0,2,1:T(8,128)S(1)}, f32[128,2,8]{0,2,1:T(8,128)S(1)}, f32[128,2,8,128]{3,0,2,1:T(8,128)}, bf16[2,128,256]{1,2,0:T(8,1...) while((s32[]{:T(128)}, f32[128,2,8]{0,2,1:T(8,128)S(1)}, ...), condition=%wide.region_5.6_spmd.clone, body=%wide.region_2.5_spmd.clone.sunk | while | flops 137122064 | bytes 7145778 | solution.py:102
  17.7 3.2 collective-permute-start
  24.7 2.8 fusion.78
  27.5 4.1 collective-permute-start
  38.0 3.8 collective-permute-start
  45.4 2.8 fusion.78
  48.1 4.0 collective-permute-start
  58.5 10.1 collective-permute-start
  75.0 9.8 collective-permute-start
  91.2 9.8 collective-permute-start
  112.2 140.4 %all-gather.3.cloned.1.call-done = bf16[1024,2048]{0,1:T(8,128)(2,1)} async-done(((bf16[128,2048]{0,1:T(8,128)(2,1)}), bf16[1024,2048]{0,1:T(8,128)(2,1)}) %all-gather.3.cloned.1.call-update) | async-done | bytes 4194320 | tf_op jit(solution)/shard_map/all_gather | solution.py:106
  252.6 4.9 multiply_reduce_fusion
  257.5 22.8 %psum.7 = f32[1024]{0:T(1024)S(1)} all-reduce(f32[1024]{0:T(1024)S(1)} %get-tuple-element.272), channel_id=1, replica_groups=mesh['ctx'=8,'exp'=32] {'ctx'}, use_global_device_ids=true, to_apply=%region_11.12 | all-reduce | flops 1024 | bytes 8192 | tf_op jit(solution)/shard_map/psum | solution.py:112
  288.7 18.7 %reduce-window.6 = s32[32,64,128]{2,1,0:T(8,128)} reduce-window(s32[32,64,128]{2,1,0:T(8,128)} %fusion.27, s32[]{:T(128)} %constant.168.clone.1), window={size=1x1x128 pad=0_0x0_0x127_0}, to_apply=%region_6.7 | reduce-window | flops 33292288 | bytes 2097156 | tf_op jit(solution)/shard_map/reduce-window
  312.9 30.6 %scatter_custom_fusion.1 = s32[2432]{0:T(1024)S(1)} fusion(s32[8192]{0:T(1024)S(1)} %broadcast_select_fusion, s32[8192]{0:T(1024)S(1)} %add_select_fusion, s32[]{:T(128)} %constant.176.clone.1), kind=kCustom, calls=%fused_computation.108 | custom fusion | bytes 9732 | tf_op jit(solution)/shard_map/broadcast_in_dim;reshape | solution.py:156
  343.8 52.4 %all-gather.5.cloned.1.call-done = bf16[1024,2048]{1,0:T(8,128)(2,1)} async-done(((bf16[1024,256]{1,0:T(8,128)(2,1)}), bf16[1024,2048]{1,0:T(8,128)(2,1)}) %all-gather.5.cloned.1.call-update) | async-done | bytes 4194320 | tf_op jit(solution)/shard_map/all_gather | solution.py:115
  396.2 4.7 concatenate.8
  400.9 22.7 %gather_fusion = bf16[2432,2048]{1,0:T(8,128)(2,1)} fusion(bf16[1025,2048]{1,0:T(8,128)(2,1)} %concatenate.8, s32[3072]{0:T(1024)S(1)} %pad_clamp_fusion), kind=kCustom, calls=%fused_computation | custom fusion | bytes 19932672 | tf_op jit(solution)/shard_map/gather | solution.py:141
  423.6 13.3 %reshape.276 = bf16[32,76,2048]{2,1,0:T(8,128)(2,1)} reshape(bf16[2432,2048]{1,0:T(8,128)(2,1)} %gather_fusion) | data formatting | bytes 19922944 | tf_op jit(solution)/shard_map/gather | solution.py:141
  436.9 238.8 %all_to_all.10 = bf16[32,76,2048]{2,1,0:T(8,128)(2,1)} all-to-all(bf16[32,76,2048]{2,1,0:T(8,128)(2,1)} %reshape.276), channel_id=1, replica_groups=mesh['ctx'=8,'exp'=32] {'exp'}, dimensions={0} | all-to-all | bytes 19922944 | tf_op jit(solution)/shard_map/all_to_all | solution.py:142
  675.7 13.3 %reshape.262 = bf16[2432,2048]{1,0:T(8,128)(2,1)} reshape(bf16[32,76,2048]{2,1,0:T(8,128)(2,1)} %all_to_all.10) | data formatting | bytes 19922944 | tf_op jit(solution)/shard_map/reshape | solution.py:143
  689.1 10.6 fusion.15
  699.7 7.8 convolution_convert_fusion
  707.5 13.3 %reshape.263 = bf16[32,76,2048]{2,1,0:T(8,128)(2,1)} reshape(bf16[2432,2048]{1,0:T(8,128)(2,1)} %convolution_convert_fusion) | data formatting | bytes 19922944 | tf_op jit(solution)/shard_map/reshape | solution.py:152
  720.8 7.2 all-to-all-start.1
  728.5 30.7 %scatter_custom_fusion.2 = f32[2432]{0:T(1024)S(1)} fusion(s32[8192]{0:T(1024)S(1)} %broadcast_select_fusion, f32[8192]{0:T(1024)S(1)} %reshape.299, f32[]{:T(128)} %constant.175.clone.1), kind=kCustom, calls=%fused_computation.106 | custom fusion | bytes 9732
  759.3 198.3 %all-to-all-done.1 = bf16[32,76,2048]{2,1,0:T(8,128)(2,1)} async-done(((bf16[32,76,2048]{2,1,0:T(8,128)(2,1)}), bf16[32,76,2048]{2,1,0:T(8,128)(2,1)}, u32[]{:S(2)}, u32[]{:S(2)}) %all-to-all-start.1) | async-done | bytes 9961504 | tf_op jit(solution)/shard_map/all_to_all | solution.py:154
  957.6 11.9 %convert_multiply_fusion = f32[32,76,2048]{2,1,0:T(8,128)} fusion(bf16[32,76,2048]{2,1,0:T(8,128)(2,1)} %all-to-all-done.1, f32[32,76]{1,0:T(8,128)S(1)} %reshape.272), kind=kLoop, calls=%fused_computation.22 | loop fusion | flops 9961472 | bytes 29894144 | tf_op jit(solution)/shard_map/mul | solution.py:155
  969.5 19.7 %reshape.287 = f32[2432,2048]{1,0:T(8,128)} reshape(f32[32,76,2048]{2,1,0:T(8,128)} %convert_multiply_fusion) | data formatting | bytes 39845888 | tf_op jit(solution)/shard_map/reshape | solution.py:157
  989.1 37.4 %scatter_custom_fusion = f32[1025,2048]{1,0:T(8,128)} fusion(s32[2432]{0:T(1024)S(1)} %scatter_custom_fusion.1, f32[2432,2048]{1,0:T(8,128)} %reshape.287, f32[]{:T(128)} %constant.175.clone.1), kind=kCustom, calls=%fused_computation.25 | custom fusion | flops 4980736 | bytes 8397312 | tf_op jit(solution)/shard_map/scatter-add | solution.py:156
  1026.5 6.0 slice.60
  1032.6 122.4 %reduce-scatter.2.cloned.1.call-done = bf16[1024,256]{1,0:T(8,128)(2,1)} async-done(((bf16[1024,2048]{1,0:T(8,128)(2,1)}), bf16[1024,256]{1,0:T(8,128)(2,1)}) %reduce-scatter.2.cloned.1.call-update) | async-done | bytes 524304 | tf_op jit(solution)/shard_map/reduce_scatter | solution.py:159
  (142 shorter events, 71.4 us)
Async XLA Ops:
  6.5 682.5 %copy-start = (bf16[1,2048,768]{2,1,0:T(8,128)(2,1)S(1)}, bf16[1,2048,768]{2,1,0:T(8,128)(2,1)}, u32[]{:S(2)}) copy-start(bf16[1,2048,768]{2,1,0:T(8,128)(2,1)} %param.18) | copy-start | bytes 9437188
  6.5 246.1 %all-gather.3.cloned.1.call-start = ((), (), s32[]{:S(2)}) async-start(), calls=%async_computation.3 | async-start | bytes 4718592 | tf_op jit(solution)/shard_map/all_gather | solution.py:106
  17.7 5.3 collective-permute-start
  27.5 6.0 collective-permute-start
  38.0 5.7 collective-permute-start
  48.1 5.9 collective-permute-start
  58.5 12.1 %collective-permute-start = (bf16[2,128,256]{1,2,0:T(8,128)(2,1)S(1)}, bf16[2,128,256]{1,2,0:T(8,128)(2,1)S(1)}, u32[]{:S(2)}, u32[]{:S(2)}) collective-permute-start(bf16[2,128,256]{1,2,0:T(8,128)(2,1)S(1)} %get-tuple-element.358), channel_id=1, source_target_pairs={{0,32},{32,64},{64,96},{96,128},{128,160},{160,192},{192,224},{1,3... | collective-permute-start | bytes 393224 | tf_op jit(solution)/shard_map/while/body/eval_jaxpr/ppermute | solution.py:17
  75.0 11.7 %collective-permute-start = (bf16[2,128,256]{1,2,0:T(8,128)(2,1)S(1)}, bf16[2,128,256]{1,2,0:T(8,128)(2,1)S(1)}, u32[]{:S(2)}, u32[]{:S(2)}) collective-permute-start(bf16[2,128,256]{1,2,0:T(8,128)(2,1)S(1)} %get-tuple-element.358), channel_id=1, source_target_pairs={{0,32},{32,64},{64,96},{96,128},{128,160},{160,192},{192,224},{1,3... | collective-permute-start | bytes 393224 | tf_op jit(solution)/shard_map/while/body/eval_jaxpr/ppermute | solution.py:17
  91.2 11.7 %collective-permute-start = (bf16[2,128,256]{1,2,0:T(8,128)(2,1)S(1)}, bf16[2,128,256]{1,2,0:T(8,128)(2,1)S(1)}, u32[]{:S(2)}, u32[]{:S(2)}) collective-permute-start(bf16[2,128,256]{1,2,0:T(8,128)(2,1)S(1)} %get-tuple-element.358), channel_id=1, source_target_pairs={{0,32},{32,64},{64,96},{96,128},{128,160},{160,192},{192,224},{1,3... | collective-permute-start | bytes 393224 | tf_op jit(solution)/shard_map/while/body/eval_jaxpr/ppermute | solution.py:17
  107.4 172.9 %copy-start.4 = (f32[256]{0:T(256)S(1)}, f32[256]{0:T(256)}, u32[]{:S(2)}) copy-start(f32[256]{0:T(256)} %param.17) | copy-start | bytes 3076
  107.4 175.2 %copy-start.2 = (s32[1,1024,8]{1,2,0:T(8,128)S(1)}, s32[1,1024,8]{1,2,0:T(8,128)}, u32[]{:S(2)}) copy-start(s32[1,1024,8]{1,2,0:T(8,128)} %param.20) | copy-start | bytes 98308
  112.2 284.0 %all-gather.5.cloned.1.call-start = ((), (), s32[]{:S(2)}) async-start(), calls=%async_computation.4 | async-start | bytes 4718592 | tf_op jit(solution)/shard_map/all_gather | solution.py:115
  257.5 55.0 %copy-start.6 = (s32[2]{0:T(128)S(1)}, s32[2]{0:T(128)}, u32[]{:S(2)}) copy-start(s32[2]{0:T(128)} %constant.200) | copy-start | bytes 28
  257.5 55.2 %copy-start.5 = (s32[2]{0:T(128)S(1)}, s32[2]{0:T(128)}, u32[]{:S(2)}) copy-start(s32[2]{0:T(128)} %constant.203) | copy-start | bytes 28
  689.1 10.7 copy-start.7
  720.8 7.2 copy-start.3
  720.8 236.7 %all-to-all-start.1 = ((bf16[32,76,2048]{2,1,0:T(8,128)(2,1)}), bf16[32,76,2048]{2,1,0:T(8,128)(2,1)}, u32[]{:S(2)}, u32[]{:S(2)}) async-start(bf16[32,76,2048]{2,1,0:T(8,128)(2,1)} %reshape.263), calls=%async_computation.1 | async-start | bytes 20971520 | tf_op jit(solution)/shard_map/all_to_all | solution.py:154
  728.0 427.0 %reduce-scatter.2.cloned.1.call-start = ((), (), s32[]{:S(2)}) async-start(), calls=%async_computation.5 | async-start | bytes 4718592 | tf_op jit(solution)/shard_map/reduce_scatter | solution.py:159
  989.1 168.1 %copy-start.1 = (bf16[1,2048,768]{2,1,0:T(8,128)(2,1)S(1)}, bf16[1,2048,768]{2,1,0:T(8,128)(2,1)}, u32[]{:S(2)}) copy-start(bf16[1,2048,768]{2,1,0:T(8,128)(2,1)} %param.18) | copy-start | bytes 9437188
Sparse Core Ops, SparseCore 0:
  112.3 140.2 all-gather.2
  282.7 113.4 all-gather.4
  1032.7 122.2 reduce-scatter.1
where the time goes:
time: 1180 us; the launch traced here: 1160 us
  waiting for transfers between devices  526 us (45%)
  blocking collectives  262 us (22%)
  local copies, waits for them, and re-layouts  173 us (15%)
  other arithmetic  81.5 us (7%)
  matrix products  55.3 us (5%)
  starting transfers between devices  52.1 us (4%)
  between operations  13.4 us (1%)
    all_to_all x1, blocking collectives, shards(): lax.all_to_all(outgoing, 'exp', split_axis=0, concat_axis=0, tiled=True)  239 us
    all_to_all x1, waiting for transfers between devices, shards(): lax.all_to_all(expert_out, 'exp', split_axis=0, concat_axis=0, tiled=True)  198 us
    all_gather x1, waiting for transfers between devices, shards(): lax.all_gather(context, 'ctx', axis=0, tiled=True)  140 us
    reduce_scatter x1, waiting for transfers between devices, shards(): lax.psum_scatter(partial_sum.astype(jnp.bfloat16), 'ctx', scatter_dimensi...  122 us
    all_gather x1, waiting for transfers between devices, shards(): normed = lax.all_gather(normed_cols, 'ctx', axis=1, tiled=True)  52.4 us
    ppermute x7, starting transfers between devices, passed_along(): return lax.ppermute(value, axis, pairs)  44.8 us
    unnamed x23, local copies, waits for them, and re-layouts  38.1 us
    scatter-add x1, other arithmetic, shards(): jax.ops.segment_sum(weighted.reshape(-1, width), token_table.reshape(-1),...  37.4 us
  transfers between devices with their start and end apart: 11, of which 11 were waited for; matrix products, arithmetic and copies ran while one was open for 8% of the time, Pallas kernels for 0%

commit v1 on v0

v1 whole, which is shorter than its diff:
```python
import jax
import jax.numpy as jnp
from jax import lax
from jax.experimental import pallas as pl
from jax.experimental.pallas import tpu as pltpu
from jax.sharding import PartitionSpec as P

LENGTH = 1024
D = 2048
HEAD = 128
TOP = 8
SLOTS = 80
BLK = 256
MESH = pl.DeviceIdType.MESH
norm_eps = 1e-06


def whole(
    q_ref, k_ref, v_ref, res_ref, w_ref, gain_ref, ids_ref, gates_ref, gu_ref, dp_ref,
    out_ref,
    kvb, cb, idb, gtb, rank, gate, tab, xb, sb, rb, gw, dw, hid, sq, ctt, rsend, rrecv,
    s_kv, r_kv, s_cx, r_cx, s_id, r_id, s_sq, r_sq, s_w, r_w, l_w, s_c, r_c2,
    s_z, r_z, s_f, r_f, s_o, r_o, s_r, r_r,
):
    ctx = lax.axis_index("ctx")
    exp = lax.axis_index("exp")
    z_hi, y = ctx // 4, ctx % 4
    z_lo, j = exp // 8, exp % 8
    x, core = j // 2, j % 2
    z = z_hi * 4 + z_lo
    mirror = (z_hi + 1) % 2 * 4 + y

    def at_z(to):
        return ((to // 4) * 4 + y, (to % 4) * 8 + j)

    def remote(src, dst, send, recv, where):
        return pltpu.make_async_remote_copy(
            src_ref=src, dst_ref=dst, send_sem=send, recv_sem=recv,
            device_id=where, device_id_type=MESH,
        )

    def bytes_of(ref, sem):
        return pltpu.make_async_copy(ref, ref, sem)

    barrier = pltpu.get_barrier_semaphore()

    def greet(where):
        pl.semaphore_signal(barrier, inc=1, device_id=where, device_id_type=MESH)

    @pl.loop(0, 32)
    def _(n):
        yy, jj = n // 8, n % 8

        @pl.when(jnp.logical_or(yy != y, jj != j))
        def _():
            greet((z_hi * 4 + yy, z_lo * 8 + jj))

    @pl.loop(1, 8)
    def _(n):
        greet(at_z((z + n) % 8))

    @pl.loop(1, 4)
    def _(n):
        greet(((z_hi + 1) % 2 * 4 + (y + n) % 4, exp))

    pl.semaphore_wait(barrier, 31 + 7 + 3)

    def id_copies(n):
        to = (ctx, (z_lo + n) % 4 * 8 + j)
        return (
            remote(ids_ref, idb.at[z_lo], s_id.at[0, n], r_id.at[0, z_lo], to),
            remote(gates_ref, gtb.at[z_lo], s_id.at[1, n], r_id.at[1, z_lo], to),
        )

    own = pl.ds(pl.multiple_of(ctx * 128, 128), 128)
    kvb[0, own, :] = k_ref[...]
    kvb[1, own, :] = v_ref[...]

    def kv_copy(slot, n, sem):
        rows = pl.ds(pl.multiple_of(slot * 128, 128), 128)
        part = kvb.at[:, rows, :]
        return remote(part, part, s_kv.at[sem], r_kv.at[slot], (z_hi * 4 + (y + n) % 4, exp))

    def kv_over():
        part = kvb.at[:, own, :]
        return remote(part, part, s_kv.at[0], r_kv.at[ctx], (mirror, exp))

    @pl.when(z_hi == 0)
    def _():
        kv_over().start()
        kvb[:, 512:1024, :] = jnp.zeros((2, 512, 256), jnp.bfloat16)

    for n in (1, 2, 3):
        kv_copy(ctx, n, n).start()
    for n in (1, 2, 3):
        for copy in id_copies(n):
            copy.start()
    idb[z_lo] = ids_ref[...]
    gtb[z_lo] = gates_ref[...]

    mine = core == y % 2
    sibling = (ctx, exp + 1 - 2 * core)
    across = (ctx + 1 - 2 * (y % 2), exp)

    def own_local():
        return (
            pltpu.make_async_copy(gu_ref, gw.at[0], l_w.at[0]),
            pltpu.make_async_copy(dp_ref, dw.at[0], l_w.at[1]),
        )

    def own_sibling():
        return (
            remote(gu_ref, gw.at[0], s_w.at[0], r_w.at[0], sibling),
            remote(dp_ref, dw.at[0], s_w.at[1], r_w.at[1], sibling),
        )

    def own_across():
        return (
            remote(gu_ref, gw.at[1], s_w.at[0], r_w.at[2], across),
            remote(dp_ref, dw.at[1], s_w.at[1], r_w.at[3], across),
        )

    def pass_sibling():
        return (
            remote(gw.at[1], gw.at[1], s_c.at[0], r_c2.at[0], sibling),
            remote(dw.at[1], dw.at[1], s_c.at[1], r_c2.at[1], sibling),
        )

    @pl.when(mine)
    def _():
        for copy in own_local() + own_sibling():
            copy.start()

    @pl.when(jnp.logical_not(mine))
    def _():
        for copy in own_across():
            copy.start()

    rrecv[0, 0, 128:256, :] = jnp.zeros((128, LENGTH), jnp.bfloat16)
    rrecv[1, 0, 0:128, :] = jnp.zeros((128, LENGTH), jnp.bfloat16)

    for n in (1, 2, 3):
        at = (z_lo + n) % 4
        bytes_of(idb.at[at], r_id.at[0, at]).wait()
        bytes_of(gtb.at[at], r_id.at[1, at]).wait()

    @pl.loop(0, 4)
    def _(s):
        number = lax.broadcasted_iota(jnp.int32, (16, LENGTH), 0)
        number = z_hi * 64 + z_lo * 8 + jnp.where(number >= 8, number + 24, number)
        found = jnp.zeros((16, LENGTH), jnp.float32)
        weight = jnp.zeros((16, LENGTH), jnp.float32)
        ids, gates = idb[s], gtb[s]
        for k in range(TOP):
            same = ids[k : k + 1, :] == number
            found = found + jnp.where(same, 1.0, 0.0)
            weight = weight + jnp.where(same, gates[k : k + 1, :], 0.0)
        rows = pl.ds(pl.multiple_of(s * 16, 16), 16)
        rank[rows, :] = found
        gate[rows, :] = weight

    members = rank[...]
    members16 = members.astype(jnp.bfloat16)
    before = []
    for b in range(8):
        row = lax.broadcasted_iota(jnp.int32, (LENGTH, 128), 0)
        column = lax.broadcasted_iota(jnp.int32, (LENGTH, 128), 1) + b * 128
        earlier = jnp.where(row < column, 1.0, 0.0).astype(jnp.bfloat16)
        before.append(jnp.dot(members16, earlier, preferred_element_type=jnp.float32))
    rank[...] = jnp.where(members > 0.5, jnp.concatenate(before, axis=1), -1.0)

    place = lambda: lax.broadcasted_iota(jnp.int32, (SLOTS, LENGTH), 0).astype(jnp.float32)

    @pl.loop(0, 64)
    def _(n):
        row = rank[pl.ds(n, 1), :]
        tab[n] = jnp.where(row == place(), 1.0, 0.0).astype(jnp.bfloat16)

    @pl.when(z_hi == 1)
    def _():
        bytes_of(kvb.at[:, pl.ds(0, 128), :], r_kv.at[mirror]).wait()
        for n in (1, 2, 3):
            kv_copy(mirror, n, 3 + n).start()

    for n in (1, 2, 3):
        bytes_of(kvb.at[:, pl.ds(0, 128), :], r_kv.at[z_hi * 4 + (y + n) % 4]).wait()

    @pl.when(z_hi == 1)
    def _():
        for n in (1, 2, 3):
            bytes_of(kvb.at[:, pl.ds(0, 128), :], r_kv.at[(y + n) % 4]).wait()

    def cx_part(g, slot):
        return cb.at[pl.ds(4 * g, 4), pl.ds(pl.multiple_of(slot * 128, 128), 128), :]

    def cx_copy(g, slot, n, sem):
        part = cx_part(g, slot)
        return remote(
            part, part, s_cx.at[g, sem], r_cx.at[g, slot], (z_hi * 4 + (y + n) % 4, exp)
        )

    def cx_over(g):
        part = cx_part(g, ctx)
        return remote(part, part, s_cx.at[g, 0], r_cx.at[g, ctx], (mirror, exp))

    def cx_wait(g, slot):
        bytes_of(cx_part(g, slot), r_cx.at[g, slot]).wait()

    for g in range(2):
        lanes = slice(g * 128, g * 128 + 128)

        @pl.loop(0, 4)
        def _(n):
            results = []
            for i in range(2):
                cols = pl.ds(pl.multiple_of((g * 8 + n * 2 + i) * 128, 128), 128)
                scores = lax.dot_general(
                    q_ref[:, cols], kvb[0, :, lanes], (((1,), (1,)), ((), ())),
                    preferred_element_type=jnp.float32,
                ) * (HEAD**-0.5)
                row = lax.broadcasted_iota(jnp.int32, (128, LENGTH), 0) + ctx * 128
                column = lax.broadcasted_iota(jnp.int32, (128, LENGTH), 1)
                scores = jnp.where(column <= row, scores, -1e30)
                top = jnp.max(scores, axis=1, keepdims=True)
                weights = jnp.exp(scores - top)
                total = jnp.sum(weights, axis=1, keepdims=True)
                mixed = jnp.dot(
                    weights.astype(jnp.bfloat16), kvb[1, :, lanes],
                    preferred_element_type=jnp.float32,
                )
                results.append((mixed / total).astype(jnp.bfloat16))
            cb[g * 4 + n, own, :] = jnp.concatenate(results, axis=1)

        cx_over(g).start()
        for n in (1, 2, 3):
            cx_copy(g, ctx, n, n).start()

    for g in range(2):
        cx_wait(g, mirror)
        for n in (1, 2, 3):
            cx_copy(g, mirror, n, 3 + n).start()
    for g in range(2):
        for n in (1, 2, 3):
            cx_wait(g, z_hi * 4 + (y + n) % 4)
    for g in range(2):
        for n in (1, 2, 3):
            cx_wait(g, (z_hi + 1) % 2 * 4 + (y + n) % 4)

    for b in range(4):
        rows = slice(b * 256, b * 256 + 256)
        total = res_ref[rows, :].astype(jnp.float32)
        for f in range(8):
            total = total + jnp.dot(
                cb[f, rows, :], w_ref[f * BLK : f * BLK + BLK, :],
                preferred_element_type=jnp.float32,
            )
        hid[rows, :] = total
        squares = total * total
        squares = squares[:, :128] + squares[:, 128:]
        sq[ctx, :, rows] = jnp.sum(squares.T, axis=0, keepdims=True)

    def sq_copy(n):
        to = (ctx + n) % 8
        return remote(sq.at[ctx], sq.at[ctx], s_sq.at[n], r_sq.at[ctx], (to, exp))

    for n in range(1, 8):
        sq_copy(n).start()
    for n in range(1, 8):
        at = (ctx + n) % 8
        bytes_of(sq.at[at], r_sq.at[at]).wait()
    total = sq[0]
    for n in range(1, 8):
        total = total + sq[n]
    inverse = lax.rsqrt(total / D + norm_eps)
    for b in range(4):
        rows = slice(b * 256, b * 256 + 256)
        column = jnp.broadcast_to(inverse[:, rows], (128, 256)).T
        column = jnp.concatenate([column, column], axis=1)
        xb[z, rows, :] = (hid[rows, :] * column * gain_ref[...]).astype(jnp.bfloat16)

    right, left = at_z((z + 1) % 8), at_z((z + 7) % 8)

    def z_right(i):
        part = xb.at[(z + 8 - i) % 8]
        if i == 3:
            part = part.at[0:512]
        return remote(part, part, s_z.at[0, i], r_z.at[0, i], right)

    def z_left(i):
        part = xb.at[(z + i) % 8]
        if i == 3:
            part = part.at[512:1024]
        return remote(part, part, s_z.at[1, i], r_z.at[1, i], left)

    def is_me(s, yy, xx):
        return jnp.logical_and(s % 2 == core, jnp.logical_and(yy == y, xx == x))

    def deal(zz):
        s, half = zz % 4, zz // 4
        col = pl.ds(pl.multiple_of((half * 4 + y) * BLK, BLK), BLK)
        to_rows = pl.ds(pl.multiple_of((s // 2 * 8 + j) * SLOTS, SLOTS), SLOTS)
        dst = rb.at[to_rows, col]

        @pl.loop(0, 4)
        def _(n):
            lhs = tab[pl.ds(s * 16 + n * 4, 4)].reshape(4 * SLOTS, LENGTH)
            rows = pl.ds(pl.multiple_of(n * 4 * SLOTS, 4 * SLOTS), 4 * SLOTS)
            sb[zz, rows, :] = jnp.dot(
                lhs, xb[zz], preferred_element_type=jnp.float32
            ).astype(jnp.bfloat16)

            @pl.loop(0, 4)
            def _(i):
                e = n * 4 + i
                yy, xx = e // 8 * 2 + e % 2, e % 8 // 2
                src = sb.at[zz, pl.ds(pl.multiple_of(e * SLOTS, SLOTS), SLOTS), :]
                same = is_me(s, yy, xx)

                @pl.when(same)
                def _():
                    pltpu.make_async_copy(src, dst, r_f.at[s // 2]).start()

                @pl.when(jnp.logical_not(same))
                def _():
                    to = (z_hi * 4 + yy, z_lo * 8 + xx * 2 + s % 2)
                    remote(src, dst, s_f.at[zz], r_f.at[s // 2], to).start()

    z_right(0).start()
    z_left(0).start()
    for g in range(2):
        cx_over(g).wait_send()
        for n in (1, 2, 3):
            cx_copy(g, ctx, n, n).wait_send()
            cx_copy(g, mirror, n, 3 + n).wait_send()
    deal(z)
    for i in range(3):
        z_right(i).wait_recv()
        z_right(i + 1).start()
        z_left(i).wait_recv()
        z_left(i + 1).start()
        deal((z + 7 - i) % 8)
        deal((z + 1 + i) % 8)
        if i == 1:

            @pl.when(mine)
            def _():
                for n in (0, 1):
                    bytes_of((gw, dw)[n].at[1], r_w.at[2 + n]).wait()
                for copy in pass_sibling():
                    copy.start()

    z_right(3).wait_recv()
    z_left(3).wait_recv()
    deal((z + 4) % 8)

    @pl.when(mine)
    def _():
        for copy in own_local():
            copy.wait()

    @pl.when(jnp.logical_not(mine))
    def _():
        for n in (0, 1):
            bytes_of((gw, dw)[n].at[0], r_w.at[n]).wait()
            bytes_of((gw, dw)[n].at[1], r_c2.at[n]).wait()

    @pl.loop(0, 8)
    def _(zz):
        some = (zz % 4) % 2 == core

        @pl.when(some)
        def _():
            bytes_of(sb.at[zz, 0 : 15 * SLOTS], s_f.at[zz]).wait()

        @pl.when(jnp.logical_not(some))
        def _():
            bytes_of(sb.at[zz], s_f.at[zz]).wait()

    def distance(zz):
        up = (zz + 8 - z) % 8
        return jnp.minimum(up, 8 - up)

    my_e = y // 2 * 8 + x * 2 + y % 2

    for p in range(2):
        bytes_of(rb.at[p * 640 : p * 640 + 640], r_f.at[p]).wait()

    for turn in range(2):
        p = (z_lo // 2 + turn) % 2
        s = 2 * p + core

        @pl.loop(0, 2)
        def _(n):
            rows = pl.ds(pl.multiple_of(p * 640 + n * 320, 320), 320)
            units = []
            for h in range(2):
                u = jnp.dot(rb[rows, :], gw[h], preferred_element_type=jnp.float32)
                v = u[:, :384]
                units.append((v / (1.0 + jnp.exp(-v)) * u[:, 384:]).astype(jnp.bfloat16))
            for f in range(8):
                cols = slice(f * BLK, f * BLK + BLK)
                sb[f, rows, :] = (
                    jnp.dot(units[0], dw[0, :, cols], preferred_element_type=jnp.float32)
                    + jnp.dot(units[1], dw[1, :, cols], preferred_element_type=jnp.float32)
                ).astype(jnp.bfloat16)

        first = jnp.where(distance(s) >= distance(4 + s), 0, 1)

        @pl.loop(0, 2)
        def _(m):
            half = (first + m) % 2
            slot = half * 4 + s
            dst = cb.at[slot, pl.ds(pl.multiple_of(my_e * SLOTS, SLOTS), SLOTS), :]

            @pl.loop(0, 32)
            def _(n):
                yy, jj = n % 4, n // 4
                from_rows = pl.ds(pl.multiple_of((p * 8 + jj) * SLOTS, SLOTS), SLOTS)
                src = sb.at[half * 4 + yy, from_rows, :]
                same = jnp.logical_and(yy == y, jj == j)

                @pl.when(same)
                def _():
                    pltpu.make_async_copy(src, dst, r_o.at[slot]).start()

                @pl.when(jnp.logical_not(same))
                def _():
                    to = (z_hi * 4 + yy, z_lo * 8 + jj)
                    remote(src, dst, s_o.at[p, half], r_o.at[slot], to).start()

    @pl.loop(0, 64)
    def _(n):
        row = rank[pl.ds(n, 1), :]
        tab[n] = jnp.where(row == place(), gate[pl.ds(n, 1), :], 0.0).astype(jnp.bfloat16)

    def turned(zz):
        bytes_of(cb.at[zz], r_o.at[zz]).wait()
        ctt[...] = cb[zz].T

    def tile(zz, t):
        rhs = tab[pl.ds(zz % 4 * 16, 16), :, t].reshape(16 * SLOTS, 256)
        return jnp.dot(ctt[...], rhs, preferred_element_type=jnp.float32)

    def tiles(body):
        @pl.loop(0, 4)
        def _(n):
            body(pl.ds(pl.multiple_of(n * 256, 256), 256))

    def r_copy(way, i):
        to = (right, left)[way]
        if i == 0:
            rows = slice(0, 128) if way == 0 else slice(128, 256)
            src, dst = rsend.at[0, 0, rows], rrecv.at[way, 0, rows]
        else:
            src, dst = rsend.at[way, i], rrecv.at[way, i]
        return remote(src, dst, s_r.at[way, i], r_r.at[way, i], to)

    far = (z + 4) % 8
    turned(far)

    def start_far(t):
        rsend[0, 0, :, t] = tile(far, t).astype(jnp.bfloat16)

    tiles(start_far)
    r_copy(0, 0).start()
    r_copy(1, 0).start()
    for i in range(1, 4):
        for way in range(2):
            zz = (z + 4 - i) % 8 if way == 0 else (z + 4 + i) % 8
            turned(zz)
            r_copy(way, i - 1).wait_recv()

            def add(t, zz=zz, way=way, i=i):
                rsend[way, i, :, t] = (
                    tile(zz, t) + rrecv[way, i - 1, :, t].astype(jnp.float32)
                ).astype(jnp.bfloat16)

            tiles(add)
            r_copy(way, i).start()
    turned(z)
    r_copy(0, 3).wait_recv()
    r_copy(1, 3).wait_recv()

    def finish(t):
        total = (
            tile(z, t)
            + rrecv[0, 3, :, t].astype(jnp.float32)
            + rrecv[1, 3, :, t].astype(jnp.float32)
        )
        out_ref[t, :] = (hid[t, :] + total.T).astype(jnp.bfloat16)

    tiles(finish)

    @pl.when(z_hi == 0)
    def _():
        kv_over().wait_send()

    @pl.when(z_hi == 1)
    def _():
        for n in (1, 2, 3):
            kv_copy(mirror, n, 3 + n).wait_send()

    for n in (1, 2, 3):
        kv_copy(ctx, n, n).wait_send()
        for copy in id_copies(n):
            copy.wait_send()
    for n in range(1, 8):
        sq_copy(n).wait_send()

    @pl.when(mine)
    def _():
        for copy in own_sibling():
            copy.wait_send()

    @pl.when(mine)
    def _():
        for copy in pass_sibling():
            copy.wait_send()

    @pl.when(jnp.logical_not(mine))
    def _():
        for copy in own_across():
            copy.wait_send()

    for i in range(4):
        z_right(i).wait_send()
        z_left(i).wait_send()
        r_copy(0, i).wait_send()
        r_copy(1, i).wait_send()
    for p in range(2):
        for half in range(2):
            bytes_of(sb.at[0:5, 0:496], s_o.at[p, half]).wait()


def shards(q, k, v, residual, w, gain, gate_up, down, ids, gates):
    vmem = pl.BlockSpec(memory_space=pltpu.VMEM)
    anywhere = pl.BlockSpec(memory_space=pl.ANY)
    bf16, f32 = jnp.bfloat16, jnp.float32
    dma = pltpu.SemaphoreType.DMA
    out = pl.pallas_call(
        whole,
        out_shape=jax.ShapeDtypeStruct((LENGTH, BLK), bf16),
        in_specs=[vmem] * 8 + [anywhere] * 2,
        out_specs=vmem,
        scratch_shapes=[
            pltpu.VMEM((2, LENGTH, 256), bf16),
            pltpu.VMEM((8, 16 * SLOTS, BLK), bf16),
            pltpu.VMEM((4, TOP, LENGTH), jnp.int32),
            pltpu.VMEM((4, TOP, LENGTH), f32),
            pltpu.VMEM((64, LENGTH), f32),
            pltpu.VMEM((64, LENGTH), f32),
            pltpu.VMEM((64, SLOTS, LENGTH), bf16),
            pltpu.VMEM((8, LENGTH, BLK), bf16),
            pltpu.VMEM((8, 16 * SLOTS, BLK), bf16),
            pltpu.VMEM((16 * SLOTS, D), bf16),
            pltpu.VMEM((2, D, 768), bf16),
            pltpu.VMEM((2, 384, D), bf16),
            pltpu.VMEM((LENGTH, BLK), f32),
            pltpu.VMEM((8, 1, LENGTH), f32),
            pltpu.VMEM((BLK, 16 * SLOTS), bf16),
            pltpu.VMEM((2, 4, BLK, LENGTH), bf16),
            pltpu.VMEM((2, 4, BLK, LENGTH), bf16),
            dma((8,)), dma((8,)), dma((2, 8)), dma((2, 8)), dma((2, 4)), dma((2, 4)),
            dma((8,)), dma((8,)), dma((2,)), dma((4,)), dma((2,)), dma((2,)), dma((2,)),
            dma((2, 4)), dma((2, 4)), dma((8,)), dma((2,)), dma((2, 2)), dma((8,)),
            dma((2, 4)), dma((2, 4)),
        ],
        compiler_params=pltpu.CompilerParams(
            collective_id=0, has_side_effects=True, vmem_limit_bytes=63 * 1024 * 1024
        ),
    )(
        q[0], k[0], v[0], residual[0], w, gain[None], ids[0].T, gates[0].T,
        gate_up[0], down[0],
    )
    return out[None]


def solution(mesh):
    return jax.shard_map(
        shards,
        mesh=mesh,
        in_specs=(
            P("exp", "ctx", None),
            P("exp", "ctx", None),
            P("exp", "ctx", None),
            P("exp", None, "ctx"),
            P(None, "ctx"),
            P("ctx"),
            P(("ctx", "exp"), None, None),
            P(("ctx", "exp"), None, None),
            P("exp", None, None),
            P("exp", None, None),
        ),
        out_specs=P("exp", None, "ctx"),
        check_vma=False,
    )
```

time: 1180 us -> 303 us (0.26)
  waiting for transfers between devices: 526 us -> 0 us
  Pallas kernels: 0 us -> 295 us
  blocking collectives: 262 us -> 0 us
  local copies, waits for them, and re-layouts: 173 us -> 1.87 us
  other arithmetic: 81.5 us -> 0 us
  matrix products: 55.3 us -> 0 us
  starting transfers between devices: 52.1 us -> 0 us
  between operations: 13.4 us -> 0.01 us
    pallas_call x0 -> x1, Pallas kernels: none -> 295 us  [shards(): pl.pallas_call(whole, out_shape=jax.ShapeDtypeStruct((LENGTH, BLK), bf16)...]
    all_to_all x1 -> x0, blocking collectives: 239 us -> none  [shards(): lax.all_to_all(outgoing, 'exp', split_axis=0, concat_axis=0, tiled=True)]
    all_to_all x1 -> x0, waiting for transfers between devices: 198 us -> none  [shards(): lax.all_to_all(expert_out, 'exp', split_axis=0, concat_axis=0, tiled=True)]
    all_gather x2 -> x0, waiting for transfers between devices: 193 us -> none  [the longest x1 140 us: shards(): lax.all_gather(context, 'ctx', axis=0, tiled=True)]
    reduce_scatter x1 -> x0, waiting for transfers between devices: 122 us -> none  [shards(): lax.psum_scatter(partial_sum.astype(jnp.bfloat16), 'ctx', scatter_dimensi...]
    dot_general x19 -> x0, matrix products: 55.3 us -> none  [the longest x8 20.8 us: attend_block(): jnp.einsum('qkgt,tkd->qkgd', weights.astype(jnp.bfloat16), values_grouped...]
    reshape x3 -> x0, local copies, waits for them, and re-layouts: 46.3 us -> none  [the longest x1 19.7 us: shards(): weighted.reshape(-1, width)]
    ppermute x7 -> x0, starting transfers between devices: 44.8 us -> none  [passed_along(): return lax.ppermute(value, axis, pairs)]
  transfers between devices with their start and end apart: 11 -> 0, of which waited for: 11 -> 0; matrix products, arithmetic and copies ran while one was open for 8% -> 0% of each run, Pallas kernels for 0% -> 0%
where the time goes in v1:
time: 303 us; the launch traced here: 297 us
  Pallas kernels  295 us (97%)
    pallas_call x1, Pallas kernels, shards(): pl.pallas_call(whole, out_shape=jax.ShapeDtypeStruct((LENGTH, BLK), bf16)...  295 us

profile of v1, /device:TPU:97, one launch (start us, length us, event | category | flops | bytes accessed | tf_op | source)
XLA Modules:
  0.0 296.9 jit_solution(2097477956127163044)
XLA Ops:
  0.0 295.0 %shard_map.100 = bf16[1024,256]{1,0:T(8,128)(2,1)} custom-call(bf16[128,2048]{1,0:T(8,128)(2,1)} %bitcast.17, bf16[128,256]{1,0:T(8,128)(2,1)} %bitcast.19, bf16[128,256]{1,0:T(8,128)(2,1)} %bitcast.20, bf16[1024,256]{1,0:T(8,128)(2,1)} %bitcast.18, bf16[2048,256]{1,0:T(8,128)(2,1)} %w_ref.1, f32[1,256]{1,0:T(1,128)} %bitcast.23, s32[8,1024]{1,0:T(8,128)} %bitcast.21, ...), custom_call_target="tpu_custom_call" | custom-call | tf_op jit(solution)/shard_map/pallas_call | solution.py:540
  295.1 1.9 copy.12

commit v2 on v1

v2 whole, which is shorter than its diff:
```python
import jax
import jax.numpy as jnp
from jax import lax
from jax.experimental import pallas as pl
from jax.experimental.pallas import tpu as pltpu
from jax.sharding import PartitionSpec as P

LENGTH = 1024
D = 2048
HEAD = 128
TOP = 8
SLOTS = 80
BLK = 256
MESH = pl.DeviceIdType.MESH
norm_eps = 1e-06


def whole(
    q_ref, k_ref, v_ref, res_ref, w_ref, gain_ref, ids_ref, gates_ref, gu_ref, dp_ref,
    out_ref,
    kvb, cb, idb, gtb, rank, gate, tab, xb, sb, rb, gw, dw, hid, sq, ctt, rsend, rrecv, wm, resm, gm, hs, hm, acc, base,
    s_kv, r_kv, s_cx, r_cx, s_wm, r_wm, s_rm, r_rm, s_id, r_id, s_sq, r_sq, s_w, r_w, l_w, s_c, r_c2,
    s_z, r_z, s_f, r_f, s_o, r_o, s_r, r_r,
):
    ctx = lax.axis_index("ctx")
    exp = lax.axis_index("exp")
    z_hi, y = ctx // 4, ctx % 4
    z_lo, j = exp // 8, exp % 8
    x, core = j // 2, j % 2
    z = z_hi * 4 + z_lo
    mirror = (z_hi + 1) % 2 * 4 + y

    def at_z(to):
        return ((to // 4) * 4 + y, (to % 4) * 8 + j)

    def remote(src, dst, send, recv, where):
        return pltpu.make_async_remote_copy(
            src_ref=src, dst_ref=dst, send_sem=send, recv_sem=recv,
            device_id=where, device_id_type=MESH,
        )

    def bytes_of(ref, sem):
        return pltpu.make_async_copy(ref, ref, sem)

    barrier = pltpu.get_barrier_semaphore()
    pending = []

    def greet(where):
        pl.semaphore_signal(barrier, inc=1, device_id=where, device_id_type=MESH)

    @pl.loop(0, 32)
    def _(n):
        yy, jj = n // 8, n % 8

        @pl.when(jnp.logical_or(yy != y, jj != j))
        def _():
            greet((z_hi * 4 + yy, z_lo * 8 + jj))

    @pl.loop(1, 8)
    def _(n):
        greet(at_z((z + n) % 8))

    pl.semaphore_wait(barrier, 31 + 7)

    def id_copies(n):
        to = (ctx, (z_lo + n) % 4 * 8 + j)
        return (
            remote(ids_ref, idb.at[z_lo], s_id.at[0, n], r_id.at[0, z_lo], to),
            remote(gates_ref, gtb.at[z_lo], s_id.at[1, n], r_id.at[1, z_lo], to),
        )

    own = pl.ds(pl.multiple_of(ctx * 128, 128), 128)
    kvb[0, own, :] = k_ref[...]
    kvb[1, own, :] = v_ref[...]

    def kv_copy(slot, n, sem):
        rows = pl.ds(pl.multiple_of(slot * 128, 128), 128)
        part = kvb.at[:, rows, :]
        return remote(part, part, s_kv.at[sem], r_kv.at[slot], (z_hi * 4 + (y + n) % 4, exp))

    def kv_over():
        part = kvb.at[:, own, :]
        return remote(part, part, s_kv.at[0], r_kv.at[ctx], (mirror, exp))

    @pl.when(z_hi == 0)
    def _():
        kv_over().start()
        kvb[:, 512:1024, :] = jnp.zeros((2, 512, 256), jnp.bfloat16)

    for n in (1, 2, 3):
        kv_copy(ctx, n, n).start()
    for n in (1, 2, 3):
        for copy in id_copies(n):
            copy.start()
    idb[z_lo] = ids_ref[...]
    gtb[z_lo] = gates_ref[...]

    def kv_sent():
        @pl.when(z_hi == 0)
        def _():
            kv_over().wait_send()

        for n in (1, 2, 3):
            kv_copy(ctx, n, n).wait_send()
            for copy in id_copies(n):
                copy.wait_send()

    pending.append(kv_sent)

    half_w = pl.ds(pl.multiple_of(core * 1024, 1024), 1024)
    here = pl.ds(pl.multiple_of(z_hi * 512, 512), 512)
    there = pl.ds(pl.multiple_of((1 - z_hi) * 512, 512), 512)
    other = (mirror, exp)

    def w_over(n):
        to = (mirror, jnp.where(z_lo == 3, n, 3 - n) * 8 + j)
        return remote(w_ref.at[half_w, :], wm.at[half_w, :], s_wm.at[n], r_wm.at[0], to)

    def w_sibling():
        return remote(
            wm.at[half_w, :], wm.at[half_w, :], s_wm.at[2], r_wm.at[1], (ctx, exp + 1 - 2 * core)
        )

    def res_over():
        return (
            remote(res_ref.at[there, :], resm, s_rm.at[0], r_rm.at[0], other),
            remote(gain_ref, gm, s_rm.at[1], r_rm.at[1], other),
        )

    @pl.when(jnp.logical_or(z_lo == 3, z_lo == 0))
    def _():
        w_over(0).start()
        w_over(1).start()

    def w_sent():
        @pl.when(jnp.logical_or(z_lo == 3, z_lo == 0))
        def _():
            w_over(0).wait_send()
            w_over(1).wait_send()

        w_sibling().wait_send()
        for copy in res_over():
            copy.wait_send()

    pending.append(w_sent)

    @pl.when(z_hi == 1)
    def _():
        for copy in res_over():
            copy.start()

    mine = core == y % 2
    sibling = (ctx, exp + 1 - 2 * core)
    across = (ctx + 1 - 2 * (y % 2), exp)

    def own_local():
        return (
            pltpu.make_async_copy(gu_ref, gw.at[0], l_w.at[0]),
            pltpu.make_async_copy(dp_ref, dw.at[0], l_w.at[1]),
        )

    def own_sibling():
        return (
            remote(gu_ref, gw.at[0], s_w.at[0], r_w.at[0], sibling),
            remote(dp_ref, dw.at[0], s_w.at[1], r_w.at[1], sibling),
        )

    cuts = (0, 1024, 1280, 2048)

    def own_across(n):
        if n == 3:
            return remote(dp_ref, dw.at[1], s_w.at[3], r_w.at[5], across)
        rows = slice(cuts[n], cuts[n + 1])
        return remote(gu_ref.at[rows], gw.at[1, rows], s_w.at[n], r_w.at[2 + n], across)

    def across_arrived():
        for n in range(3):
            bytes_of(gw.at[1, cuts[n] : cuts[n + 1]], r_w.at[2 + n]).wait()
        bytes_of(dw.at[1], r_w.at[5]).wait()

    def send_across(*which):
        @pl.when(jnp.logical_not(mine))
        def _():
            for n in which:
                own_across(n).start()

    def pass_sibling():
        return (
            remote(gw.at[1], gw.at[1], s_c.at[0], r_c2.at[0], sibling),
            remote(dw.at[1], dw.at[1], s_c.at[1], r_c2.at[1], sibling),
        )

    @pl.when(mine)
    def _():
        for copy in own_local() + own_sibling():
            copy.start()

    send_across(0)

    def weights_sent():
        @pl.when(mine)
        def _():
            for copy in own_sibling():
                copy.wait_send()

        @pl.when(jnp.logical_not(mine))
        def _():
            for n in range(4):
                own_across(n).wait_send()

    pending.append(weights_sent)

    rrecv[0, 0, 128:256, :] = jnp.zeros((128, LENGTH), jnp.bfloat16)
    rrecv[1, 0, 0:128, :] = jnp.zeros((128, LENGTH), jnp.bfloat16)

    for n in (1, 2, 3):
        at = (z_lo + n) % 4
        bytes_of(idb.at[at], r_id.at[0, at]).wait()
        bytes_of(gtb.at[at], r_id.at[1, at]).wait()

    @pl.loop(0, 4)
    def _(s):
        number = lax.broadcasted_iota(jnp.int32, (16, LENGTH), 0)
        number = z_hi * 64 + z_lo * 8 + jnp.where(number >= 8, number + 24, number)
        found = jnp.zeros((16, LENGTH), jnp.float32)
        weight = jnp.zeros((16, LENGTH), jnp.float32)
        ids, gates = idb[s], gtb[s]
        for k in range(TOP):
            same = ids[k : k + 1, :] == number
            found = found + jnp.where(same, 1.0, 0.0)
            weight = weight + jnp.where(same, gates[k : k + 1, :], 0.0)
        rows = pl.ds(pl.multiple_of(s * 16, 16), 16)
        rank[rows, :] = found
        gate[rows, :] = weight

    members = rank[...]
    members16 = members.astype(jnp.bfloat16)
    before = []
    for b in range(8):
        row = lax.broadcasted_iota(jnp.int32, (LENGTH, 128), 0)
        column = lax.broadcasted_iota(jnp.int32, (LENGTH, 128), 1) + b * 128
        earlier = jnp.where(row < column, 1.0, 0.0).astype(jnp.bfloat16)
        before.append(jnp.dot(members16, earlier, preferred_element_type=jnp.float32))
    rank[...] = jnp.where(members > 0.5, jnp.concatenate(before, axis=1), -1.0)

    place = lambda: lax.broadcasted_iota(jnp.int32, (SLOTS, LENGTH), 0).astype(jnp.float32)

    @pl.loop(0, 64)
    def _(n):
        row = rank[pl.ds(n, 1), :]
        tab[n] = jnp.where(row == place(), 1.0, 0.0).astype(jnp.bfloat16)

    @pl.when(z_hi == 1)
    def _():
        bytes_of(kvb.at[:, pl.ds(0, 128), :], r_kv.at[mirror]).wait()
        for n in (1, 2, 3):
            kv_copy(mirror, n, 3 + n).start()

    def kv_passed():
        @pl.when(z_hi == 1)
        def _():
            for n in (1, 2, 3):
                kv_copy(mirror, n, 3 + n).wait_send()

    pending.append(kv_passed)

    for n in (1, 2, 3):
        bytes_of(kvb.at[:, pl.ds(0, 128), :], r_kv.at[z_hi * 4 + (y + n) % 4]).wait()

    @pl.when(z_hi == 1)
    def _():
        for n in (1, 2, 3):
            bytes_of(kvb.at[:, pl.ds(0, 128), :], r_kv.at[(y + n) % 4]).wait()

    send_across(1)

    @pl.when(z_hi == 0)
    def _():
        for copy in res_over():
            copy.start()

    def cx_part(g, n, first=0, count=4):
        rows = pl.ds(pl.multiple_of((y + n) % 4 * 128, 128), 128)
        return cb.at[pl.ds(4 * g + first, count), rows, :]

    def cx_copy(g, way):
        if way < 2:
            part = cx_part(g, 0)
        elif way == 2:
            part = cx_part(g, 3, 0, 2)
        else:
            part = cx_part(g, 1, 2, 2)
        to = (z_hi * 4 + (y + (1 if way % 2 == 0 else 3)) % 4, exp)
        return remote(part, part, s_cx.at[g, way], r_cx.at[g, way], to)

    for g in range(2):
        lanes = slice(g * 128, g * 128 + 128)

        @pl.loop(0, 4)
        def _(n):
            results = []
            for i in range(2):
                cols = pl.ds(pl.multiple_of((g * 8 + n * 2 + i) * 128, 128), 128)
                scores = lax.dot_general(
                    q_ref[:, cols], kvb[0, :, lanes], (((1,), (1,)), ((), ())),
                    preferred_element_type=jnp.float32,
                ) * (HEAD**-0.5)
                row = lax.broadcasted_iota(jnp.int32, (128, LENGTH), 0) + ctx * 128
                column = lax.broadcasted_iota(jnp.int32, (128, LENGTH), 1)
                scores = jnp.where(column <= row, scores, -1e30)
                top = jnp.max(scores, axis=1, keepdims=True)
                weights = jnp.exp(scores - top)
                total = jnp.sum(weights, axis=1, keepdims=True)
                mixed = jnp.dot(
                    weights.astype(jnp.bfloat16), kvb[1, :, lanes],
                    preferred_element_type=jnp.float32,
                )
                results.append((mixed / total).astype(jnp.bfloat16))
            cb[g * 4 + n, pl.ds(pl.multiple_of(y * 128, 128), 128), :] = jnp.concatenate(results, axis=1)

        cx_copy(g, 0).start()
        cx_copy(g, 1).start()

    bytes_of(wm.at[half_w, :], r_wm.at[0]).wait()
    w_sibling().start()
    for g in range(2):
        for way in range(2):
            cx_copy(g, way).wait_recv()
            cx_copy(g, 2 + way).start()
    for g in range(2):
        for way in (2, 3):
            cx_copy(g, way).wait_recv()

    bytes_of(resm, r_rm.at[0]).wait()
    bytes_of(gm, r_rm.at[1]).wait()
    bytes_of(wm.at[half_w, :], r_wm.at[1]).wait()
    for b in range(2):
        rows = slice(b * 256, b * 256 + 256)
        mine_rows = pl.ds(pl.multiple_of(z_hi * 512 + b * 256, 256), 256)
        squares = jnp.zeros((256, 128), jnp.float32)
        for side, weight in enumerate((w_ref, wm)):
            total = (res_ref[mine_rows, :] if side == 0 else resm[rows, :]).astype(jnp.float32)
            for f in range(8):
                total = total + jnp.dot(
                    cb[f, rows, :], weight[f * BLK : f * BLK + BLK, :],
                    preferred_element_type=jnp.float32,
                )
            hid[side, rows, :] = total
            squared = total * total
            squares = squares + (squared[:, :128] + squared[:, 128:])
        sq[y, :, rows] = jnp.sum(squares.T, axis=0, keepdims=True)

    def sq_copy(n):
        to = (z_hi * 4 + (y + n) % 4, exp)
        return remote(sq.at[y], sq.at[y], s_sq.at[n], r_sq.at[y], to)

    for n in (1, 2, 3):
        sq_copy(n).start()
        pending.append(sq_copy(n).wait_send)
    send_across(2, 3)
    hs[...] = hid[1].astype(jnp.bfloat16)
    for n in (1, 2, 3):
        at = (y + n) % 4
        bytes_of(sq.at[at], r_sq.at[at]).wait()
    total = sq[0] + sq[1] + (sq[2] + sq[3])
    inverse = lax.rsqrt(total / D + norm_eps)
    for b in range(2):
        rows = slice(b * 256, b * 256 + 256)
        column = jnp.broadcast_to(inverse[:, rows], (128, 256)).T
        column = jnp.concatenate([column, column], axis=1)
        for side, gains in enumerate((gain_ref, gm)):
            xb[z_hi if side == 0 else 1 - z_hi, z, rows, :] = (
                hid[side, rows, :] * column * gains[...]
            ).astype(jnp.bfloat16)

    def hid_over():
        return remote(hs, hm, s_rm.at[2], r_rm.at[2], other)

    right, left = at_z((z + 1) % 8), at_z((z + 7) % 8)

    def z_copy(way, i, half):
        block = (z + 8 - i) % 8 if way == 0 else (z + i) % 8
        part = xb.at[half, block]
        if i == 3:
            part = part.at[0:256] if way == 0 else part.at[256:512]
        to = (right, left)[way]
        return remote(part, part, s_z.at[way, i, half], r_z.at[way, i, half], to)

    def is_me(s, yy, xx):
        return jnp.logical_and(s % 2 == core, jnp.logical_and(yy == y, xx == x))

    def deal(s, half):
        to_rows = pl.ds(pl.multiple_of((s // 2 * 8 + j) * SLOTS, SLOTS), SLOTS)
        dst = rb.at[to_rows, pl.ds(pl.multiple_of((half * 4 + y) * BLK, BLK), BLK)]
        zz = half * 4 + s

        @pl.loop(0, 4)
        def _(turn):
            n = (turn + y // 2 * 2 + x // 2) % 4
            lhs = tab[pl.ds(s * 16 + n * 4, 4)].reshape(4 * SLOTS, LENGTH)
            rows = pl.ds(pl.multiple_of(n * 4 * SLOTS, 4 * SLOTS), 4 * SLOTS)
            sb[zz, rows, :] = (
                jnp.dot(lhs[:, :512], xb[half, s], preferred_element_type=jnp.float32)
                + jnp.dot(lhs[:, 512:], xb[half, 4 + s], preferred_element_type=jnp.float32)
            ).astype(jnp.bfloat16)

            @pl.loop(0, 4)
            def _(i):
                e = n * 4 + (i + x % 2 * 2 + y % 2) % 4
                yy, xx = e // 8 * 2 + e % 2, e % 8 // 2
                src = sb.at[zz, pl.ds(pl.multiple_of(e * SLOTS, SLOTS), SLOTS), :]
                same = is_me(s, yy, xx)

                @pl.when(same)
                def _():
                    pltpu.make_async_copy(src, dst, r_f.at[s // 2]).start()

                @pl.when(jnp.logical_not(same))
                def _():
                    to = (z_hi * 4 + yy, z_lo * 8 + xx * 2 + s % 2)
                    remote(src, dst, s_f.at[zz], r_f.at[s // 2], to).start()

    for half in range(2):
        for way in range(2):
            z_copy(way, 0, half).start()
            pending += [z_copy(way, i, half).wait_send for i in range(4)]
    for g in range(2):
        for way in range(4):
            cx_copy(g, way).wait_send()
    for i in range(3):
        for half in range(2):
            for way in range(2):
                z_copy(way, i, half).wait_recv()
                z_copy(way, i + 1, half).start()
            if i == 1:
                deal((z_lo + 2) % 4, half)
            if i == 2:
                deal((z_lo + 1) % 4, half)
    for half in range(2):
        z_copy(0, 3, half).wait_recv()
        z_copy(1, 3, half).wait_recv()
        deal(z_lo, half)
    for half in range(2):
        deal((z_lo + 3) % 4, half)
    hid_over().start()
    pending.append(hid_over().wait_send)

    @pl.when(mine)
    def _():
        across_arrived()
        for copy in pass_sibling():
            copy.start()

    def weights_passed():
        @pl.when(mine)
        def _():
            for copy in pass_sibling():
                copy.wait_send()

    pending.append(weights_passed)
    @pl.when(mine)
    def _():
        for copy in own_local():
            copy.wait()

    @pl.when(jnp.logical_not(mine))
    def _():
        for n in (0, 1):
            bytes_of((gw, dw)[n].at[0], r_w.at[n]).wait()
            bytes_of((gw, dw)[n].at[1], r_c2.at[n]).wait()

    def dealt():
        @pl.loop(0, 8)
        def _(zz):
            some = (zz % 4) % 2 == core

            @pl.when(some)
            def _():
                bytes_of(sb.at[zz, 0 : 15 * SLOTS], s_f.at[zz]).wait()

            @pl.when(jnp.logical_not(some))
            def _():
                bytes_of(sb.at[zz], s_f.at[zz]).wait()

    pending.append(dealt)

    def distance(zz):
        up = (zz + 8 - z) % 8
        return jnp.minimum(up, 8 - up)

    my_e = y // 2 * 8 + x * 2 + y % 2

    def send_back(p, half, n):
        slot = half * 4 + 2 * p + core
        dst = cb.at[slot, pl.ds(pl.multiple_of(my_e * SLOTS, SLOTS), SLOTS), :]

        @pl.loop(0, 16)
        def _(m):
            yy, jj = (m + y) % 4, n * 4 + (m // 4 + x % 2 * 2 + core) % 4
            from_rows = pl.ds(pl.multiple_of((p * 8 + jj) * SLOTS, SLOTS), SLOTS)
            col = pl.ds(pl.multiple_of((half * 4 + yy) * BLK, BLK), BLK)
            src = rb.at[from_rows, col]
            same = jnp.logical_and(yy == y, jj == j)

            @pl.when(same)
            def _():
                pltpu.make_async_copy(src, dst, r_o.at[slot]).start()

            @pl.when(jnp.logical_not(same))
            def _():
                to = (z_hi * 4 + yy, z_lo * 8 + jj)
                remote(src, dst, s_o.at[p, half], r_o.at[slot], to).start()

    plain = core == z_lo % 2

    def far_half(p):
        s = 2 * p + core
        return jnp.where(distance(s) >= distance(4 + s), 0, 1)

    for turn in range(2):
        p = (z_lo // 2 + 1 + turn) % 2
        bytes_of(rb.at[pl.ds(pl.multiple_of(p * 640, 640), 640)], r_f.at[p]).wait()

        @pl.loop(0, 2)
        def _(m):
            n = (m + x // 2) % 2
            rows = pl.ds(pl.multiple_of(p * 640 + n * 320, 320), 320)
            units = []
            for h in range(2):
                u = jnp.dot(rb[rows, :], gw[h], preferred_element_type=jnp.float32)
                v = u[:, :384]
                units.append((v / (1.0 + jnp.exp(-v)) * u[:, 384:]).astype(jnp.bfloat16))

            def results(half):
                for i in range(4):
                    cols = pl.ds(pl.multiple_of((half * 4 + i) * BLK, BLK), BLK)
                    rb[rows, cols] = (
                        jnp.dot(units[0], dw[0, :, cols], preferred_element_type=jnp.float32)
                        + jnp.dot(units[1], dw[1, :, cols], preferred_element_type=jnp.float32)
                    ).astype(jnp.bfloat16)

            first = far_half(p)
            results(first)
            if turn == 1:
                send_back(p, first, n)
            else:

                @pl.when(jnp.logical_not(plain))
                def _():
                    send_back(p, first, n)

            results(1 - first)

    def send_both(p, half):
        @pl.loop(0, 2)
        def _(m):
            send_back(p, half, (m + x // 2) % 2)

    early, late = (z_lo // 2 + 1) % 2, z_lo // 2

    @pl.when(plain)
    def _():
        send_both(early, far_half(early))

    send_both(early, 1 - far_half(early))
    send_both(late, 1 - far_half(late))

    for p in range(2):
        for half in range(2):
            pending.append(bytes_of(sb.at[0:5, 0:496], s_o.at[p, half]).wait)

    @pl.loop(0, 64)
    def _(n):
        row = rank[pl.ds(n, 1), :]
        tab[n] = jnp.where(row == place(), gate[pl.ds(n, 1), :], 0.0).astype(jnp.bfloat16)

    def turned(zz):
        bytes_of(cb.at[zz], r_o.at[zz]).wait()
        ctt[...] = cb[zz].T

    def tile(zz, t):
        rhs = tab[pl.ds(zz % 4 * 16, 16), :, t].reshape(16 * SLOTS, 256)
        return jnp.dot(ctt[...], rhs, preferred_element_type=jnp.float32)

    def tiles(body):
        @pl.loop(0, 4)
        def _(n):
            body(pl.ds(pl.multiple_of(n * 256, 256), 256))

    def r_copy(way, i):
        to = (right, left)[way]
        if i == 0:
            rows = slice(0, 128) if way == 0 else slice(128, 256)
            src, dst = rsend.at[0, 0, rows], rrecv.at[way, 0, rows]
        else:
            src, dst = rsend.at[way, i], rrecv.at[way, i]
        return remote(src, dst, s_r.at[way, i], r_r.at[way, i], to)

    for i in range(4):
        pending += [r_copy(0, i).wait_send, r_copy(1, i).wait_send]
    far = (z + 4) % 8
    turned(far)

    def start_far(t):
        rsend[0, 0, :, t] = tile(far, t).astype(jnp.bfloat16)

    tiles(start_far)
    r_copy(0, 0).start()
    r_copy(1, 0).start()
    for i in range(1, 4):
        for way in range(2):
            zz = (z + 4 - i) % 8 if way == 0 else (z + 4 + i) % 8
            turned(zz)

            def keep(t, zz=zz):
                acc[:, t] = tile(zz, t)

            def add(t, way=way, i=i):
                rsend[way, i, :, t] = (
                    acc[:, t] + rrecv[way, i - 1, :, t].astype(jnp.float32)
                ).astype(jnp.bfloat16)

            tiles(keep)
            r_copy(way, i - 1).wait_recv()
            tiles(add)
            r_copy(way, i).start()
    turned(z)
    hid_over().wait_recv()

    def start(t, before):
        base[t, :] = before + tile(z, t).T

    @pl.loop(0, 2)
    def _(n):
        rows = pl.ds(pl.multiple_of(n * 256, 256), 256)
        start(pl.ds(pl.multiple_of(z_hi * 512 + n * 256, 256), 256), hid[0, rows, :])
        start(
            pl.ds(pl.multiple_of((1 - z_hi) * 512 + n * 256, 256), 256),
            hm[rows, :].astype(jnp.float32),
        )

    r_copy(0, 3).wait_recv()
    r_copy(1, 3).wait_recv()

    @tiles
    def _(t):
        arrived = rrecv[0, 3, :, t].astype(jnp.float32) + rrecv[1, 3, :, t].astype(jnp.float32)
        out_ref[t, :] = (base[t, :] + arrived.T).astype(jnp.bfloat16)


    for check in pending:
        check()


def shards(q, k, v, residual, w, gain, gate_up, down, ids, gates):
    vmem = pl.BlockSpec(memory_space=pltpu.VMEM)
    anywhere = pl.BlockSpec(memory_space=pl.ANY)
    bf16, f32 = jnp.bfloat16, jnp.float32
    dma = pltpu.SemaphoreType.DMA
    out = pl.pallas_call(
        whole,
        out_shape=jax.ShapeDtypeStruct((LENGTH, BLK), bf16),
        in_specs=[vmem] * 8 + [anywhere] * 2,
        out_specs=vmem,
        scratch_shapes=[
            pltpu.VMEM((2, LENGTH, 256), bf16),
            pltpu.VMEM((8, 16 * SLOTS, BLK), bf16),
            pltpu.VMEM((4, TOP, LENGTH), jnp.int32),
            pltpu.VMEM((4, TOP, LENGTH), f32),
            pltpu.VMEM((64, LENGTH), f32),
            pltpu.VMEM((64, LENGTH), f32),
            pltpu.VMEM((64, SLOTS, LENGTH), bf16),
            pltpu.VMEM((2, 8, 512, BLK), bf16),
            pltpu.VMEM((8, 16 * SLOTS, BLK), bf16),
            pltpu.VMEM((16 * SLOTS, D), bf16),
            pltpu.VMEM((2, D, 768), bf16),
            pltpu.VMEM((2, 384, D), bf16),
            pltpu.VMEM((2, 512, BLK), f32),
            pltpu.VMEM((4, 1, 512), f32),
            pltpu.VMEM((BLK, 16 * SLOTS), bf16),
            pltpu.VMEM((2, 4, BLK, LENGTH), bf16),
            pltpu.VMEM((2, 4, BLK, LENGTH), bf16),
            pltpu.VMEM((D, BLK), bf16),
            pltpu.VMEM((512, BLK), bf16),
            pltpu.VMEM((1, BLK), f32),
            pltpu.VMEM((512, BLK), bf16),
            pltpu.VMEM((512, BLK), bf16),
            pltpu.VMEM((BLK, LENGTH), f32),
            pltpu.VMEM((LENGTH, BLK), f32),
            dma((8,)), dma((8,)), dma((2, 4)), dma((2, 4)), dma((3,)), dma((2,)), dma((3,)), dma((3,)),
            dma((2, 4)), dma((2, 4)),
            dma((8,)), dma((8,)), dma((4,)), dma((6,)), dma((2,)), dma((2,)), dma((2,)),
            dma((2, 4, 2)), dma((2, 4, 2)), dma((8,)), dma((2,)), dma((2, 2)), dma((8,)),
            dma((2, 4)), dma((2, 4)),
        ],
        compiler_params=pltpu.CompilerParams(
            collective_id=0, has_side_effects=True, vmem_limit_bytes=63 * 1024 * 1024
        ),
    )(
        q[0], k[0], v[0], residual[0], w, gain[None], ids[0].T, gates[0].T,
        gate_up[0], down[0],
    )
    return out[None]


def solution(mesh):
    return jax.shard_map(
        shards,
        mesh=mesh,
        in_specs=(
            P("exp", "ctx", None),
            P("exp", "ctx", None),
            P("exp", "ctx", None),
            P("exp", None, "ctx"),
            P(None, "ctx"),
            P("ctx"),
            P(("ctx", "exp"), None, None),
            P(("ctx", "exp"), None, None),
            P("exp", None, None),
            P("exp", None, None),
        ),
        out_specs=P("exp", None, "ctx"),
        check_vma=False,
    )
```

time: 303 us -> 244 us (0.81); the launches traced: 297 us -> 244 us
  Pallas kernels: 295 us -> 242 us
    pallas_call x1, Pallas kernels: 295 us -> 242 us  [shards(): pl.pallas_call(whole, out_shape=jax.ShapeDtypeStruct((LENGTH, BLK), bf16)...]
where the time goes in v2:
time: 244 us
  Pallas kernels  242 us (99%)
    pallas_call x1, Pallas kernels, shards(): pl.pallas_call(whole, out_shape=jax.ShapeDtypeStruct((LENGTH, BLK), bf16)...  242 us

profile of v2, /device:TPU:97, one launch (start us, length us, event | category | flops | bytes accessed | tf_op | source)
XLA Modules:
  0.0 244.1 jit_solution(4597983830044206422)
XLA Ops:
  0.0 242.2 %shard_map.100 = bf16[1024,256]{1,0:T(8,128)(2,1)} custom-call(bf16[128,2048]{1,0:T(8,128)(2,1)} %bitcast.17, bf16[128,256]{1,0:T(8,128)(2,1)} %bitcast.19, bf16[128,256]{1,0:T(8,128)(2,1)} %bitcast.20, bf16[1024,256]{1,0:T(8,128)(2,1)} %bitcast.18, bf16[2048,256]{1,0:T(8,128)(2,1)} %w_ref.1, f32[1,256]{1,0:T(1,128)} %bitcast.23, s32[8,1024]{1,0:T(8,128)} %bitcast.21, ...), custom_call_target="tpu_custom_call" | custom-call | tf_op jit(solution)/shard_map/pallas_call | solution.py:660
  242.2 1.9 copy.12

commit v3 on v2

--- a/solution.py
+++ b/solution.py
@@ -127,11 +127,6 @@
             remote(gain_ref, gm, s_rm.at[1], r_rm.at[1], other),
         )
 
-    @pl.when(jnp.logical_or(z_lo == 3, z_lo == 0))
-    def _():
-        w_over(0).start()
-        w_over(1).start()
-
     def w_sent():
         @pl.when(jnp.logical_or(z_lo == 3, z_lo == 0))
         def _():
@@ -144,11 +139,6 @@
 
     pending.append(w_sent)
 
-    @pl.when(z_hi == 1)
-    def _():
-        for copy in res_over():
-            copy.start()
-
     mine = core == y % 2
     sibling = (ctx, exp + 1 - 2 * core)
     across = (ctx + 1 - 2 * (y % 2), exp)
@@ -217,6 +207,16 @@
         at = (z_lo + n) % 4
         bytes_of(idb.at[at], r_id.at[0, at]).wait()
         bytes_of(gtb.at[at], r_id.at[1, at]).wait()
+
+    @pl.when(jnp.logical_or(z_lo == 3, z_lo == 0))
+    def _():
+        w_over(0).start()
+        w_over(1).start()
+
+    @pl.when(z_hi == 1)
+    def _():
+        for copy in res_over():
+            copy.start()
 
     @pl.loop(0, 4)
     def _(s):
@@ -321,12 +321,12 @@
         cx_copy(g, 0).start()
         cx_copy(g, 1).start()
 
-    bytes_of(wm.at[half_w, :], r_wm.at[0]).wait()
-    w_sibling().start()
     for g in range(2):
         for way in range(2):
             cx_copy(g, way).wait_recv()
             cx_copy(g, 2 + way).start()
+    bytes_of(wm.at[half_w, :], r_wm.at[0]).wait()
+    w_sibling().start()
     for g in range(2):
         for way in (2, 3):
             cx_copy(g, way).wait_recv()

time: 244 us -> 245 us (level)
  no operation moved by 1% of the time
where the time goes in v3:
time: 245 us; the launch traced here: 244 us
  Pallas kernels  242 us (99%)
    pallas_call x1, Pallas kernels, shards(): pl.pallas_call(whole, out_shape=jax.ShapeDtypeStruct((LENGTH, BLK), bf16)...  242 us

profile of v3, /device:TPU:97, one launch (start us, length us, event | category | flops | bytes accessed | tf_op | source)
XLA Modules:
  0.0 244.3 jit_solution(17718679839922533613)
XLA Ops:
  0.0 242.4 %shard_map.100 = bf16[1024,256]{1,0:T(8,128)(2,1)} custom-call(bf16[128,2048]{1,0:T(8,128)(2,1)} %bitcast.17, bf16[128,256]{1,0:T(8,128)(2,1)} %bitcast.19, bf16[128,256]{1,0:T(8,128)(2,1)} %bitcast.20, bf16[1024,256]{1,0:T(8,128)(2,1)} %bitcast.18, bf16[2048,256]{1,0:T(8,128)(2,1)} %w_ref.1, f32[1,256]{1,0:T(1,128)} %bitcast.23, s32[8,1024]{1,0:T(8,128)} %bitcast.21, ...), custom_call_target="tpu_custom_call" | custom-call | tf_op jit(solution)/shard_map/pallas_call | solution.py:660
  242.4 1.9 copy.12
